TPU v7x, 512 devices: a whole 4x8x8 slice. The times are simulated.
512 devices in a mesh: rep: 64 (over y_hi, z, x), fsdp: 8 (over y_lo, core).
Axes of the slice: x: 4, y: 8 (y_hi: 2, y_lo: 4; y = y_hi * 4 + y_lo), z: 8, core: 2. Of those that a mesh axis runs over, the one named last changes fastest.
Arguments:
- tokens: bfloat16 [64, 1024, 8192], P('rep', 'fsdp'), may hold values from -6 to 6
- master: float32 [64, 3, 64, 8192], P('rep', None, None, 'fsdp'), may hold values from -4 to 4
- first_moment: float32 [64, 3, 64, 8192], P('rep', None, None, 'fsdp'), may hold values from -0.002 to 0.002
- second_moment: float32 [64, 3, 64, 8192], P('rep', None, None, 'fsdp'), may hold values from 3e-09 to 3e-08
- step_counter: int32 [1], replicated, may hold values from 1000 to 99999
Outputs:
- mixed: bfloat16 [64, 3, 64, 8192], P('rep', None, None, 'fsdp')
All inputs are finite; a program needn't handle non-finite values.
Results may differ from a plain program's by a relative error of at most 0.0056.
The roundings to bfloat16 on the way count: a program that leaves them out, or rounds other values in their place, can miss the bound.
Values may be sent and summed in bfloat16 or wider, within the bound.
A program may use at most 64 MiB of HBM per device.

v0:
```python
import functools
import math

import jax
import jax.numpy as jnp
from jax import lax
from jax.experimental import pallas as pl
from jax.experimental.pallas import tpu as pltpu
from jax.sharding import PartitionSpec as P

MESH = pl.DeviceIdType.MESH
F32 = jnp.float32
BF16 = jnp.bfloat16
NT = (((1,), (1,)), ((), ()))
CHUNK = 128
LATER = 4
LEAD = 2


def dot(a, b):
    return jnp.dot(a, b, preferred_element_type=F32)


def dot_nt(a, b):
    return lax.dot_general(a, b, NT, preferred_element_type=F32)


def split(x):
    hi = x.astype(BF16)
    return hi, (x - hi.astype(F32)).astype(BF16)


def kernel(
    bit, step, tokens, master, moment, square, out,
    tok, tok_edge, wts, acc, own, mom, sqr, part, part_in, proj, back, back_in, gram, gram_in,
    fac, fac_edge, mine, other,
    tok_sem, tok_send, tok_recv, t_send, t_recv, mas_sem, opt_sem, w_send, w_recv,
    p_sem, b_sem, m_sem, f_sem, g_send, g_recv, s_send, s_recv, o_sem,
):
    rep = lax.axis_index("rep")
    me = lax.axis_index("fsdp")
    chunks, _, hid, _ = own.shape
    cols = chunks * CHUNK
    rows = 3 * hid
    near = tokens.shape[1]
    both = 2 * near
    width = cols * lax.axis_size("fsdp")
    tok_rep = near * lax.axis_size("fsdp")
    scale_in = float(width) ** -0.5
    scale_hid = float(hid) ** -0.5

    home = me // 2
    core = me % 2
    low = home < 2
    edge = jnp.logical_or(home == 0, home == 3)
    inner = jnp.logical_not(edge)
    way = jnp.where(low, 0, 1)
    forward = jnp.where(low, me + 2, me - 2)
    backward = jnp.where(low, me - 2, me + 2)
    sibling = me + 1 - 2 * core
    mate = jnp.where((rep // 2**bit) % 2 == 0, rep + 2**bit, rep - 2**bit)

    def slot(j):
        return jnp.where(low, j, 3 - j)

    barrier = pltpu.get_barrier_semaphore()

    def greet(r, f):
        pl.semaphore_signal(barrier, inc=1, device_id=(r, f), device_id_type=MESH)

    greet(rep, sibling)
    greet(rep, forward)
    greet(mate, me)

    @pl.when(edge)
    def _():
        greet(rep, forward + 1 - 2 * core)

    @pl.when(inner)
    def _():
        greet(rep, backward)
        greet(rep, backward + 1 - 2 * core)

    def remote(src, dst, send, recv, to, r=rep):
        return pltpu.make_async_remote_copy(
            src_ref=src, dst_ref=dst, send_sem=send, recv_sem=recv,
            device_id=(r, to), device_id_type=MESH,
        )

    def columns(f, c):
        return pl.ds(pl.multiple_of(f * cols + c * CHUNK, CHUNK), CHUNK)

    near_rows = pl.ds(pl.multiple_of(core * near, near), near)

    def mas_copy(c):
        return pltpu.make_async_copy(
            master.at[0, :, :, columns(0, c)], own.at[c], mas_sem.at[c]
        )

    def tok_copy(j, c):
        return pltpu.make_async_copy(
            tokens.at[0, :, columns(2 * j + core, c)], tok.at[j, c, near_rows], tok_sem.at[j, c]
        )

    def tok_remote(j, c):
        return remote(
            tokens.at[0, :, columns(2 * j + 1 - core, c)], tok.at[j, c, near_rows],
            tok_send.at[j, c], tok_recv.at[j, c], sibling,
        )

    def t_copy(k, c, source):
        there = pl.ds(pl.multiple_of(source * near, near), near)
        return remote(
            tokens.at[0, :, columns(2 * slot(1) + k, c)], tok_edge.at[c, there],
            t_send.at[k, c], t_recv.at[source, c], 2 * slot(1) + k,
        )

    def w_copy(j, c, to):
        return remote(wts.at[j, c], wts.at[j, c], w_send.at[j, c], w_recv.at[j, c], to)

    def g_copy(d, j, c, to):
        return remote(
            acc.at[d, j, c], acc.at[d, j, c], g_send.at[d, j, c], g_recv.at[d, j, c], to
        )

    def s_copy(c):
        return remote(mine.at[c], other.at[c], s_send.at[c], s_recv.at[c], me, mate)

    def o_copy(c):
        return pltpu.make_async_copy(other.at[c], out.at[0, :, :, columns(0, c)], o_sem.at[c])

    p_copy = remote(part, part_in, p_sem.at[0], p_sem.at[1], sibling)
    b_copy = remote(back, back_in, b_sem.at[0], b_sem.at[1], backward)
    m_copy = remote(gram, gram_in, m_sem.at[0], m_sem.at[1], backward)
    tok_cols = pl.ds(0, both)
    f_copy = remote(
        fac.at[:, tok_cols], fac_edge.at[:, tok_cols], f_sem.at[0], f_sem.at[1], forward
    )
    opt_copies = (
        pltpu.make_async_copy(moment.at[0], mom, opt_sem.at[0]),
        pltpu.make_async_copy(square.at[0], sqr, opt_sem.at[1]),
    )

    def each(count):
        def run(body):
            lax.fori_loop(0, count, lambda i, c: (body(i), c)[1], 0)

        return run

    def used(j):
        return jnp.logical_or(inner, j != slot(1))

    @each(chunks)
    def _(c):
        mas_copy(c).start()

    @each(4 * chunks)
    def _(i):
        j, c = slot(i // chunks), i % chunks

        @pl.when(used(j))
        def _():
            tok_copy(j, c).start()

    for copy in opt_copies:
        copy.start()

    pl.semaphore_wait(barrier, jnp.where(edge, 4, 5))

    @each(chunks)
    def _(c):
        mas_copy(c).wait()
        wts[home, c] = own[c].reshape(rows, CHUNK).astype(BF16)
        w_copy(home, c, forward).start()

    @each(4 * chunks)
    def _(i):
        j, c = (home + i // chunks) % 4, i % chunks

        @pl.when(used(j))
        def _():
            tok_remote(j, c).start()

    @pl.when(edge)
    def _():
        @each(2 * chunks)
        def _(i):
            t_copy(i % 2, i // 2, core).start()

    part[...] = jnp.zeros_like(part)
    proj[...] = jnp.zeros_like(proj)
    for f in (fac, fac_edge):
        f[pl.ds(0, 2 * hid), pl.ds(both, 2 * hid)] = jnp.zeros((2 * hid, 2 * hid), BF16)

    @pl.when(edge)
    def _():
        @each(4)
        def _(j):
            acc[way, j] = jnp.zeros(acc.shape[2:], BF16)

    def project(j, c):
        tok_copy(j, c).wait()
        tok_remote(j, c).wait_recv()
        down = wts[j, c, pl.ds(2 * hid, hid)]
        tok[j, c, pl.ds(both, hid)] = down
        tok[j, c, pl.ds(both + hid, hid)] = down
        part[:, pl.ds(0, both + hid)] += dot_nt(wts[j, c], tok[j, c, pl.ds(0, both + hid)])

    @each(chunks)
    def _(c):
        project(home, c)

    down_rows = pl.ds(2 * hid, hid)
    gram_cols = pl.ds(both, hid)

    @pl.when(inner)
    def _():
        hi, lo = split(part[down_rows, gram_cols])
        gram[:, 0:hid] = hi
        gram[:, hid : 2 * hid] = lo
        m_copy.start()

    @each(2 * chunks)
    def _(n):
        early = n < chunks
        c = n % chunks
        j = slot(jnp.where(early, 2, 3))

        @pl.when(jnp.logical_and(inner, early))
        def _():
            w_copy(slot(0), c, forward).wait_recv()
            w_copy(slot(0), c, forward).start()

        w_copy(j, c, backward).wait_recv()

        @pl.when(inner)
        def _():
            w_copy(j, c, backward).start()

        project(j, c)

        @pl.when(jnp.logical_and(inner, early))
        def _():
            project(slot(0), c)

        @pl.when(jnp.logical_and(inner, jnp.logical_not(early)))
        def _():
            for source in range(2):
                t_copy(core, c, source).wait_recv()
            down = wts[home, c, down_rows]
            tok_edge[c, pl.ds(both, hid)] = down
            tok_edge[c, pl.ds(both + hid, hid)] = down
            proj[...] += dot_nt(wts[home, c], tok_edge[c, pl.ds(0, both)])

    @pl.when(inner)
    def _():
        back[...] = proj[...].astype(BF16)
        b_copy.start()

    @pl.when(edge)
    def _():
        m_copy.wait_recv()
        part[down_rows, gram_cols] += (
            gram_in[:, 0:hid].astype(F32) + gram_in[:, hid : 2 * hid].astype(F32)
        )
        b_copy.wait_recv()
        part[:, tok_cols] += back_in[...].astype(F32)

    p_copy.start()
    p_copy.wait_recv()

    def summed(m, c):
        here = pl.ds(m * hid, hid)
        return part[here, c] + part_in[here, c]

    gate = scale_in * summed(0, tok_cols)
    up = scale_in * summed(1, tok_cols)
    sig = jax.nn.sigmoid(gate)
    act = gate * sig
    hidden = (act * up).astype(BF16)
    wwt_hi, wwt_lo = split(summed(2, gram_cols))
    through = dot(wwt_hi, hidden) + dot(wwt_lo, hidden)
    dhidden = (scale_hid / tok_rep) * (summed(2, tok_cols) + scale_hid * through)
    fac[0:hid, 0:both] = (dhidden * up * (sig * (1.0 + gate * (1.0 - sig)))).astype(BF16)
    fac[hid : 2 * hid, 0:both] = (dhidden * act).astype(BF16)
    fac[2 * hid : rows, 0:both] = hidden

    def moments(f, h):
        hi, lo = split(scale_hid * dot_nt(h, h))
        f[2 * hid : rows, both : both + hid] = hi
        f[2 * hid : rows, both + hid : both + 2 * hid] = lo

    moments(fac, hidden)

    t = jnp.full((8, 128), step[0].astype(F32) + 1.0, F32)
    fix1 = (1.0 / (1.0 - jnp.exp(t * math.log(0.9))))[0:1, 0:1]
    fix2 = (1.0 / (1.0 - jnp.exp(t * math.log(0.999))))[0:1, 0:1]

    for copy in opt_copies:
        copy.wait()

    lag = LEAD + jnp.where(edge, chunks, 1)

    @each(2 * chunks + LEAD + LATER)
    def _(i):
        f = i - lag
        due = jnp.logical_and(f >= 0, f < chunks)

        @each(3)
        def _(q):
            going = q < 2
            c = i - jnp.where(q == 0, 0, jnp.where(going, LEAD, 1))
            j = slot(jnp.where(going, 3 - q, 0))
            d = jnp.where(going, way, 1 - way)
            to = jnp.where(going, forward, backward)

            mine_too = jnp.logical_or(going, inner)

            @pl.when(jnp.logical_and(mine_too, jnp.logical_and(c >= 0, c < chunks)))
            def _():
                @pl.when(inner)
                def _():
                    g_copy(d, j, c, to).wait_recv()

                g = dot(fac[...], tok[j, c])
                acc[d, j, c] = (g + acc[d, j, c].astype(F32)).astype(BF16)
                g_copy(d, j, c, to).start()

        @pl.when(jnp.logical_and(edge, i == 1))
        def _():
            f_copy.start()

        @pl.when(jnp.logical_and(inner, f == 0))
        def _():
            f_copy.wait_recv()
            moments(fac_edge, fac_edge[down_rows, tok_cols])

        @pl.when(due)
        def _():
            proj[:, pl.ds(0, CHUNK)] = dot(fac[...], tok[home, f])

            @pl.when(inner)
            def _():
                proj[:, pl.ds(0, CHUNK)] += dot(fac_edge[...], tok_edge[f])

            g_copy(1 - way, home, f, forward).wait_recv()
            for m in range(3):
                here = pl.ds(m * hid, hid)
                g = proj[here, pl.ds(0, CHUNK)] + acc[1 - way, home, f, here].astype(F32)
                g = g * (scale_in if m < 2 else scale_hid / tok_rep)
                param = own[f, m]
                first = (0.9 * mom[m, :, columns(0, f)] + 0.1 * g) * fix1
                second = (0.999 * sqr[m, :, columns(0, f)] + (0.001 * g) * g) * fix2
                new = param - 0.05 * (first / (jnp.sqrt(second) + 1e-8) + 0.1 * param)
                mine[f, m] = new.astype(BF16)
            s_copy(f).start()

        b = f - LATER

        @pl.when(jnp.logical_and(b >= 0, b < chunks))
        def _():
            s_copy(b).wait_recv()
            other[b] = (0.5 * (mine[b].astype(F32) + other[b].astype(F32))).astype(BF16)
            o_copy(b).start()

    p_copy.wait_send()

    @pl.when(edge)
    def _():
        f_copy.wait_send()

    @pl.when(inner)
    def _():
        m_copy.wait_send()
        b_copy.wait_send()

    @each(4 * chunks)
    def _(i):
        j, c = slot(i // chunks), i % chunks

        @pl.when(used(j))
        def _():
            tok_remote(j, c).wait_send()

        @pl.when(jnp.logical_or(inner, j == home))
        def _():
            w_copy(j, c, forward).wait_send()

    @each(chunks)
    def _(c):
        s_copy(c).wait_send()
        o_copy(c).wait()
        g_copy(way, slot(3), c, forward).wait_send()
        g_copy(way, slot(2), c, forward).wait_send()

        @pl.when(edge)
        def _():
            for k in range(2):
                t_copy(k, c, core).wait_send()

        @pl.when(inner)
        def _():
            g_copy(1 - way, slot(0), c, backward).wait_send()


def step_with(bit, tokens, master, moment, square, step):
    near = tokens.shape[1]
    hid, cols = master.shape[2:]
    rows = 3 * hid
    chunks = cols // CHUNK
    both = 2 * near
    wide = both + 2 * hid
    dma = pltpu.SemaphoreType.DMA
    anywhere = pl.BlockSpec(memory_space=pl.ANY)
    return pl.pallas_call(
        functools.partial(kernel, bit),
        out_shape=jax.ShapeDtypeStruct(master.shape, BF16),
        in_specs=[pl.BlockSpec(memory_space=pltpu.SMEM)] + [anywhere] * 4,
        out_specs=anywhere,
        scratch_shapes=[
            pltpu.VMEM((4, chunks, wide, CHUNK), BF16),
            pltpu.VMEM((chunks, wide, CHUNK), BF16),
            pltpu.VMEM((4, chunks, rows, CHUNK), BF16),
            pltpu.VMEM((2, 4, chunks, rows, CHUNK), BF16),
            pltpu.VMEM((chunks, 3, hid, CHUNK), F32),
            pltpu.VMEM((3, hid, cols), F32),
            pltpu.VMEM((3, hid, cols), F32),
            pltpu.VMEM((rows, wide), F32),
            pltpu.VMEM((rows, wide), F32),
            pltpu.VMEM((rows, both), F32),
            pltpu.VMEM((rows, both), BF16),
            pltpu.VMEM((rows, both), BF16),
            pltpu.VMEM((hid, 2 * hid), BF16),
            pltpu.VMEM((hid, 2 * hid), BF16),
            pltpu.VMEM((rows, wide), BF16),
            pltpu.VMEM((rows, wide), BF16),
            pltpu.VMEM((chunks, 3, hid, CHUNK), BF16),
            pltpu.VMEM((chunks, 3, hid, CHUNK), BF16),
            dma((4, chunks)), dma((4, chunks)), dma((4, chunks)),
            dma((2, chunks)), dma((2, chunks)),
            dma((chunks,)), dma((2,)),
            dma((4, chunks)), dma((4, chunks)),
            dma((2,)), dma((2,)), dma((2,)), dma((2,)),
            dma((2, 4, chunks)), dma((2, 4, chunks)),
            dma((chunks,)), dma((chunks,)), dma((chunks,)),
        ],
        compiler_params=pltpu.CompilerParams(
            collective_id=bit, has_side_effects=True, vmem_limit_bytes=40 * 2**20
        ),
        name=f"step_bit{bit}",
    )(step, tokens, master, moment, square)


def per_device(tokens, master, first_moment, second_moment, step_counter):
    bit_count = min(5, lax.axis_size("rep").bit_length() - 1)
    branches = [functools.partial(step_with, bit) for bit in range(bit_count)]
    return lax.switch(
        step_counter[0] % bit_count,
        branches, tokens, master, first_moment, second_moment, step_counter,
    )


def solution(mesh):
    sharded = P("rep", None, None, "fsdp")
    return jax.shard_map(
        per_device,
        mesh=mesh,
        in_specs=(P("rep", "fsdp", None), sharded, sharded, sharded, P()),
        out_specs=sharded,
        check_vma=False,
    )
```

profile of v0, /device:TPU:8, one launch (start us, length us, event | category | flops | bytes accessed | tf_op | source)
XLA Modules:
  0.0 70.8 jit_solution(16089267253159850995)
XLA Ops:
  0.7 69.4 %conditional.1 = (bf16[1,3,64,1024]{3,2,1,0:T(8,128)(2,1)S(1)}) conditional(s32[]{:T(128)} %clamp.3, (s32[1]{0:T(128)}, bf16[1,128,8192]{2,1,0:T(8,128)(2,1)}, f32[1,3,64,1024]{3,2,1,0:T(8,128)}, f32[1,3,64,1024]{3,2,1,0:T(8,128)}, f32[1,3,64,1024]{3,2,1,0:T(8,128)}) %tuple.20, (s32[1]{0:T(128)}, ...), branch_computations={%region_0.1_spmd, %region_1.2_spmd, %region_2.3_spmd, %region_3.4_... | conditional | bytes 8 | solution.py:457
  0.7 69.4 %step_bit1.1 = bf16[1,3,64,1024]{3,2,1,0:T(8,128)(2,1)S(1)} custom-call(s32[1]{0:T(128)} %get-tuple-element.66.step, bf16[1,128,8192]{2,1,0:T(8,128)(2,1)} %get-tuple-element.108.tokens, f32[1,3,64,1024]{3,2,1,0:T(8,128)} %get-tuple-element.113.master, f32[1,3,64,1024]{3,2,1,0:T(8,128)} %get-tuple-element.118.moment, ...), custom_call_target="tpu_custom_call" | custom-call | tf_op jit(solution)/shard_map/cond/branch_1_fun/step_bit1/pallas_call | solution.py:415
  70.1 0.7 %copy.38 = bf16[1,3,64,1024]{3,2,1,0:T(8,128)(2,1)} copy(bf16[1,3,64,1024]{3,2,1,0:T(8,128)(2,1)S(1)} %get-tuple-element.86) | data formatting | bytes 786432
where the time goes:
time: 71 us; the launch traced here: 70.8 us
  Pallas kernels  69.4 us (98%)
  local copies, waits for them, and re-layouts  0.75 us (1%)
    pallas_call x1, Pallas kernels, step_with(): pl.pallas_call(functools.partial(kernel, bit), out_shape=jax.ShapeDtypeSt...  69.4 us

commit v1 on v0

--- a/solution.py
+++ b/solution.py
@@ -12,9 +12,9 @@
 F32 = jnp.float32
 BF16 = jnp.bfloat16
 NT = (((1,), (1,)), ((), ()))
-CHUNK = 128
-LATER = 4
-LEAD = 2
+CHUNK = 256
+LATER = 3
+LEAD = 1
 
 
 def dot(a, b):

time: 71 us -> 67.5 us (0.951)
  the two profiles are of different devices: /device:TPU:8 before, /device:TPU:1 now
where the time goes in v1:
time: 67.5 us; the launch traced here: 67.9 us
  Pallas kernels  66.4 us (98%)
  local copies, waits for them, and re-layouts  0.75 us (1%)
  between operations  0.68 us (1%)
    pallas_call x1, Pallas kernels, step_with(): pl.pallas_call(functools.partial(kernel, bit), out_shape=jax.ShapeDtypeSt...  66.4 us

profile of v1, /device:TPU:1, one launch (start us, length us, event | category | flops | bytes accessed | tf_op | source)
XLA Modules:
  0.0 67.9 jit_solution(14149204328180518239)
XLA Ops:
  0.7 66.4 %conditional.1 = (bf16[1,3,64,1024]{3,2,1,0:T(8,128)(2,1)S(1)}) conditional(s32[]{:T(128)} %clamp.3, (s32[1]{0:T(128)}, bf16[1,128,8192]{2,1,0:T(8,128)(2,1)}, f32[1,3,64,1024]{3,2,1,0:T(8,128)}, f32[1,3,64,1024]{3,2,1,0:T(8,128)}, f32[1,3,64,1024]{3,2,1,0:T(8,128)}) %tuple.20, (s32[1]{0:T(128)}, ...), branch_computations={%region_0.1_spmd, %region_1.2_spmd, %region_2.3_spmd, %region_3.4_... | conditional | bytes 8 | solution.py:457
  0.7 66.4 %step_bit1.1 = bf16[1,3,64,1024]{3,2,1,0:T(8,128)(2,1)S(1)} custom-call(s32[1]{0:T(128)} %get-tuple-element.66.step, bf16[1,128,8192]{2,1,0:T(8,128)(2,1)} %get-tuple-element.108.tokens, f32[1,3,64,1024]{3,2,1,0:T(8,128)} %get-tuple-element.113.master, f32[1,3,64,1024]{3,2,1,0:T(8,128)} %get-tuple-element.118.moment, ...), custom_call_target="tpu_custom_call" | custom-call | tf_op jit(solution)/shard_map/cond/branch_1_fun/step_bit1/pallas_call | solution.py:415
  67.1 0.7 %copy.38 = bf16[1,3,64,1024]{3,2,1,0:T(8,128)(2,1)} copy(bf16[1,3,64,1024]{3,2,1,0:T(8,128)(2,1)S(1)} %get-tuple-element.86) | data formatting | bytes 786432
